TPU v7x, 32 devices: a whole 2x2x4 slice. The times are simulated.
32 devices in a mesh: cells: 16 (over z, x, core), species: 2 (over y).
Axes of the slice: x: 2, y: 2, z: 4, core: 2. Of those that a mesh axis runs over, the one named last changes fastest.
Arguments:
- covariates: bfloat16 [64, 256, 1024], P(None, 'cells'), may hold values from -6 to 6
- coefficients: bfloat16 [64, 8192], P('cells', 'species'), may hold values from -0.75 to 0.75
- intercept: float32 [8192], P('species'), may hold values from -6 to 6
- traits: bfloat16 [8192, 32], P('species'), may hold values from -6 to 6
- land_weight: int32 [256, 1024], P('cells'), may hold values from 0 to 3
Outputs:
- smoothed: float32 [32, 256, 1024], P('species', 'cells')
All inputs are finite; a program needn't handle non-finite values.
Results may differ from a plain program's by a relative error of at most 0.0015.
Values may be sent and summed in bfloat16 or wider, within the bound.
A program may use at most 64 MiB of HBM per device.

v0:
```python
import functools

import jax
import jax.numpy as jnp
from jax import lax
from jax.experimental import pallas as pl
from jax.experimental.pallas import tpu as pltpu
from jax.sharding import PartitionSpec as P

SWEEPS = 8
F32 = jnp.float32
BF16 = jnp.bfloat16


def sums_kernel(per, rows_per_group, cov_ref, w_ref, trait_ref, *out_refs):
    blocks, trait_rows, block_len = trait_ref.shape
    cells = cov_ref[...]

    def total(presence_of):
        acc = jnp.zeros((trait_rows, cells.shape[1]), F32)
        for j in range(blocks):
            half = jnp.dot(
                w_ref[j * block_len : (j + 1) * block_len, :], cells, preferred_element_type=F32
            )
            presence = presence_of(half).astype(BF16)
            acc = acc + jnp.dot(trait_ref[j], presence, preferred_element_type=F32)
        return acc

    def put(acc):
        for g, out_ref in enumerate(out_refs):
            out_ref[0] = acc[g * rows_per_group : (g + 1) * rows_per_group]

    acc = total(lambda half: 0.5 * jnp.tanh(half) + 0.5)
    put(acc)
    rare = jnp.min(acc[per : per + 1, :]) < blocks * block_len / 64.0

    @pl.when(rare)
    def _():
        put(total(lambda half: 1.0 / (1.0 + jnp.exp(-2.0 * half))))


def species_sums(cov_ext, w, trait_blocks, first, count, cols, per, groups, rows_per_group):
    depth = cov_ext.shape[0]
    species = w.shape[0]
    out = jax.ShapeDtypeStruct((count, rows_per_group, cols), F32)
    return pl.pallas_call(
        functools.partial(sums_kernel, per, rows_per_group),
        grid=(count,),
        in_specs=[
            pl.BlockSpec((depth, cols), lambda i: (0, i + first)),
            pl.BlockSpec(w.shape, lambda i: (0, 0)),
            pl.BlockSpec(trait_blocks.shape, lambda i: (0, 0, 0)),
        ],
        out_specs=[pl.BlockSpec((1, rows_per_group, cols), lambda i: (i, 0, 0))] * groups,
        out_shape=[out] * groups,
        compiler_params=pltpu.CompilerParams(vmem_limit_bytes=40 << 20),
        cost_estimate=pl.CostEstimate(
            flops=2 * species * 512 * cols * count,
            bytes_accessed=4 * groups * rows_per_group * cols * count,
            transcendentals=species * cols * count,
        ),
    )(cov_ext, w, trait_blocks)


def smooth_kernel(starts, land_ref, gain_ref, inverse_ref, *refs):
    mean_refs = refs[: len(starts)]
    out_ref, base, even, odd = refs[len(starts) :]
    ext, per, cols = base.shape
    column = lax.broadcasted_iota(jnp.int32, (1, cols), 1)
    not_first = (column > 0).astype(F32)
    not_last = (column < cols - 1).astype(F32)

    def around(held, r):
        here = held[r]
        sides = pltpu.roll(here, 1, 1) * not_first + pltpu.roll(here, cols - 1, 1) * not_last
        return (held[r - 1] + held[r + 1]) + sides

    for start, mean_ref in zip(starts, mean_refs):

        @pl.loop(0, mean_ref.shape[0])
        def _(i):
            r = start + i
            scaled = mean_ref[i] * land_ref[r]
            even[r] = scaled
            base[r] = scaled * inverse_ref[r]

    for sweep in range(1, SWEEPS):
        source, target = (even, odd) if sweep % 2 else (odd, even)

        @pl.loop(sweep, ext - sweep, unroll=4 if (ext - 2 * sweep) % 4 == 0 else 2)
        def _(r):
            target[r] = base[r] + gain_ref[r] * around(source, r)

    source = odd if SWEEPS % 2 == 0 else even
    for start, mean_ref in zip(starts, mean_refs):
        if SWEEPS <= start < ext - SWEEPS:

            @pl.loop(0, mean_ref.shape[0])
            def _(i):
                r = start + i
                out_ref[r - SWEEPS] = (
                    mean_ref[i] + land_ref[r] * around(source, r)
                ) * inverse_ref[r]


def gather_kernel(count, block_ref, out_ref, send_sem, recv_sem):
    me = lax.axis_index("cells")
    peers = [lax.rem(me + shift, count) for shift in range(1, count)]
    barrier = pltpu.get_barrier_semaphore()
    for peer in peers:
        pl.semaphore_signal(
            barrier, inc=1, device_id={"cells": peer}, device_id_type=pl.DeviceIdType.MESH
        )
    pl.semaphore_wait(barrier, count - 1)
    copies = [
        pltpu.make_async_remote_copy(
            src_ref=block_ref,
            dst_ref=out_ref.at[me],
            send_sem=send_sem.at[slot],
            recv_sem=recv_sem.at[slot],
            device_id={"cells": peer},
            device_id_type=pl.DeviceIdType.MESH,
        )
        for slot, peer in enumerate(peers)
    ]
    for copy in copies:
        copy.start()
    out_ref[me] = block_ref[...]
    for copy in copies:
        copy.wait()


def gather(coefficients, count):
    own, species = coefficients.shape
    tile = 16
    folds = max(1, tile // own)
    while (species // folds) % 128:
        folds //= 2
    width = species // folds
    block = coefficients.reshape(own, folds, width).transpose(1, 0, 2).reshape(own * folds, width)
    filled = -(-own * folds // tile) * tile
    block = jnp.pad(block, ((0, filled - own * folds), (0, 0)))
    blocks = pl.pallas_call(
        functools.partial(gather_kernel, count),
        out_shape=jax.ShapeDtypeStruct((count, filled, width), BF16),
        in_specs=[pl.BlockSpec(memory_space=pltpu.VMEM)],
        out_specs=pl.BlockSpec(memory_space=pltpu.VMEM),
        scratch_shapes=[pltpu.SemaphoreType.DMA((count - 1,))] * 2,
        compiler_params=pltpu.CompilerParams(collective_id=0, has_side_effects=True),
    )(block)
    blocks = blocks[:, : own * folds].reshape(count, folds, own, width)
    return blocks.transpose(0, 2, 1, 3).reshape(count * own, species)


def local(covariates, coefficients, intercept, traits, land_weight):
    ncov, rows, cols = covariates.shape
    species, trait_count = traits.shape
    groups = lax.axis_size("species")
    count = lax.axis_size("cells")
    per = trait_count // groups
    rows_per_group = -(-(per + 1) // 8) * 8
    ahead = [(i, i + 1) for i in range(count - 1)]
    back = [(target, source) for source, target in ahead]

    gathered = gather(coefficients, count)
    rounded = functools.partial(lax.reduce_precision, exponent_bits=8, mantissa_bits=7)
    bias = 0.5 * intercept
    high = rounded(bias)
    middle = rounded(bias - high)
    low = bias - high - middle
    spare = 13
    w = jnp.concatenate(
        [
            gathered * jnp.asarray(0.5, BF16),
            jnp.stack([high, middle, low]).astype(BF16),
            jnp.zeros((spare, species), BF16),
        ]
    ).T
    cov_ext = jnp.concatenate(
        [
            covariates.reshape(ncov, rows * cols),
            jnp.ones((3, rows * cols), BF16),
            jnp.zeros((spare, rows * cols), BF16),
        ]
    )
    grouped = jnp.roll(traits.T.reshape(groups, per, species), -lax.axis_index("species"), axis=0)
    grouped = jnp.concatenate(
        [
            grouped,
            jnp.ones((groups, 1, species), BF16),
            jnp.zeros((groups, rows_per_group - per - 1, species), BF16),
        ],
        axis=1,
    )
    block_len = min(512, species)
    trait_blocks = grouped.reshape(
        groups * rows_per_group, species // block_len, block_len
    ).transpose(1, 0, 2)

    below = lax.ppermute(land_weight[-SWEEPS:], "cells", ahead)
    above = lax.ppermute(land_weight[:SWEEPS], "cells", back)
    land = jnp.concatenate([below, land_weight, above]).astype(F32)
    padded = jnp.pad(land, 1)
    inverse = 1.0 / (
        1.0
        + land * (padded[2:, 1:-1] + padded[:-2, 1:-1] + padded[1:-1, 2:] + padded[1:-1, :-2])
    )
    gain = land * land * inverse

    last = 3 if rows - SWEEPS > 3 else 0
    chunks = [(0, SWEEPS), (SWEEPS, rows - SWEEPS - last), (rows - last, last)]
    own, halo = {}, {}
    for first, size in [c for c in chunks if c[1]]:
        sums = species_sums(
            cov_ext, w, trait_blocks, first, size, cols, per, groups, rows_per_group
        )
        whole = sums[0]
        for shift in range(1, groups):
            perm = [(i, (i + shift) % groups) for i in range(groups)]
            whole = whole + lax.ppermute(sums[shift], "species", perm)
        mean = whole[:, :per] / whole[:, per : per + 1]
        own[SWEEPS + first] = mean
        if first < SWEEPS:
            halo[SWEEPS + rows + first] = lax.ppermute(mean, "cells", back)
        if first >= rows - SWEEPS:
            halo[first - (rows - SWEEPS)] = lax.ppermute(mean, "cells", ahead)
    parts = {**own, **halo}
    starts = sorted(parts)
    ext = rows + 2 * SWEEPS
    smoothed = pl.pallas_call(
        functools.partial(smooth_kernel, starts),
        out_shape=jax.ShapeDtypeStruct((rows, per, cols), F32),
        scratch_shapes=[pltpu.VMEM((ext, per, cols), F32)] * 3,
        compiler_params=pltpu.CompilerParams(vmem_limit_bytes=40 << 20),
    )(land[:, None], gain[:, None], inverse[:, None], *[parts[s] for s in starts])
    return smoothed.transpose(1, 0, 2)


def solution(mesh):
    return jax.shard_map(
        local,
        mesh=mesh,
        in_specs=(
            P(None, "cells", None),
            P("cells", "species"),
            P("species"),
            P("species", None),
            P("cells", None),
        ),
        out_specs=P("species", "cells", None),
        check_vma=False,
    )
```

profile of v0, /device:TPU:1, one launch (start us, length us, event | category | flops | bytes accessed | tf_op | source)
XLA Modules:
  0.0 145.3 jit_solution(14060319911552368164)
XLA Ops:
  0.0 0.1 pad.7.clone
  0.1 0.1 pad.6.clone
  0.2 1.0 fusion
  1.2 0.0 copy-start.3
  1.2 0.1 maximum_maximum_fusion.1
  1.4 0.1 copy.28
  1.5 0.1 copy.33
  1.6 1.6 %stack.17 = bf16[1,4096]{0,1:T(8,128)(2,1)} reshape(bf16[4096]{0:T(1024)(128)(2,1)S(1)} %get-tuple-element.23) | data formatting | bytes 16384 | tf_op jit(solution)/shard_map/stack | solution.py:175
  3.2 1.6 %stack.18 = bf16[1,4096]{0,1:T(8,128)(2,1)} reshape(bf16[4096]{0:T(1024)(128)(2,1)S(1)} %get-tuple-element.22) | data formatting | bytes 16384 | tf_op jit(solution)/shard_map/stack | solution.py:175
  4.8 1.6 %stack.19 = bf16[1,4096]{0,1:T(8,128)(2,1)} reshape(bf16[4096]{0:T(1024)(128)(2,1)S(1)} %get-tuple-element.21) | data formatting | bytes 16384 | tf_op jit(solution)/shard_map/stack | solution.py:175
  6.4 0.6 reshape.65.block_ref
  7.1 16.0 %shard_map.55 = bf16[16,16,1024]{2,1,0:T(8,128)(2,1)} custom-call(bf16[16,1024]{1,0:T(8,128)(2,1)} %reshape.65.block_ref), custom_call_target="tpu_custom_call" | custom-call | tf_op jit(solution)/shard_map/pallas_call | solution.py:143
  23.1 1.1 broadcast_multiply_fusion
  24.2 0.0 copy-start.1
  24.2 0.2 mul.35
  24.4 0.3 copy.15
  24.6 0.2 copy.27
  24.8 1.3 copy.16
  26.1 1.2 copy.26
  27.4 0.1 pad.11.clone
  27.4 0.1 pad.12.clone
  27.5 0.6 maximum_maximum_fusion.cov_ref
  28.1 1.1 broadcast_in_dim.26
  29.2 6.7 %concatenate.38 = bf16[80,4096]{0,1:T(8,128)(2,1)} concatenate(bf16[64,4096]{0,1:T(8,128)(2,1)} %copy.16, bf16[1,4096]{0,1:T(8,128)(2,1)} %stack.17, bf16[1,4096]{0,1:T(8,128)(2,1)} %stack.18, bf16[1,4096]{0,1:T(8,128)(2,1)} %stack.19, bf16[13,4096]{0,1:T(8,128)(2,1)} %broadcast_in_dim.26), dimensions={0} | concatenate | bytes 1310720 | tf_op jit(solution)/shard_map/concatenate | solution.py:172
  35.9 1.2 copy-done
  37.1 30.8 %shard_map.58 = (f32[8,24,1024]{2,1,0:T(8,128)S(1)}, f32[8,24,1024]{2,1,0:T(8,128)S(1)}) custom-call(bf16[80,16384]{1,0:T(8,128)(2,1)S(1)} %maximum_maximum_fusion.cov_ref, bf16[4096,80]{1,0:T(8,128)(2,1)S(1)} %bitcast.35, bf16[8,48,512]{2,1,0:T(8,128)(2,1)S(1)} %bitcast.38), custom_call_target="tpu_custom_call" | custom-call | flops 34359738368 | bytes 1572864 | tf_op jit(solution)/shard_map/pallas_call | solution.py:46
  67.9 1.3 collective-permute-start.6
  69.3 11.6 %shard_map.57 = (f32[3,24,1024]{2,1,0:T(8,128)S(1)}, f32[3,24,1024]{2,1,0:T(8,128)S(1)}) custom-call(bf16[80,16384]{1,0:T(8,128)(2,1)S(1)} %maximum_maximum_fusion.cov_ref, bf16[4096,80]{1,0:T(8,128)(2,1)S(1)} %bitcast.36, bf16[8,48,512]{2,1,0:T(8,128)(2,1)S(1)} %bitcast.39), custom_call_target="tpu_custom_call" | custom-call | flops 12884901888 | bytes 589824 | tf_op jit(solution)/shard_map/pallas_call | solution.py:46
  80.9 0.0 copy-start.2
  80.9 0.3 collective-permute-start.4
  81.2 19.3 %shard_map.56 = (f32[5,24,1024]{2,1,0:T(8,128)S(1)}, f32[5,24,1024]{2,1,0:T(8,128)S(1)}) custom-call(bf16[80,16384]{1,0:T(8,128)(2,1)S(1)} %maximum_maximum_fusion.cov_ref, bf16[4096,80]{1,0:T(8,128)(2,1)S(1)} %bitcast.37, bf16[8,48,512]{2,1,0:T(8,128)(2,1)S(1)} %bitcast.40), custom_call_target="tpu_custom_call" | custom-call | flops 21474836480 | bytes 983040 | tf_op jit(solution)/shard_map/pallas_call | solution.py:46
  100.5 1.2 collective-permute-start.2
  101.8 5.1 %collective-permute-start = (s32[8,1024]{1,0:T(8,128)S(1)}, s32[8,1024]{1,0:T(8,128)S(1)}, u32[]{:S(2)}, u32[]{:S(2)}) collective-permute-start(s32[8,1024]{1,0:T(8,128)S(1)} %get-tuple-element.19), channel_id=1, source_target_pairs={{0,2},{2,4},{4,6},{6,8},{8,10},{10,12},{12,14},{14,16},{16,18},{18... | collective-permute-start | bytes 98312 | tf_op jit(solution)/shard_map/ppermute | solution.py:200
  106.8 1.9 %collective-permute-start.1 = (s32[8,1024]{1,0:T(8,128)S(1)}, s32[8,1024]{1,0:T(8,128)S(1)}, u32[]{:S(2)}, u32[]{:S(2)}) collective-permute-start(s32[8,1024]{1,0:T(8,128)S(1)} %get-tuple-element.20), channel_id=1, source_target_pairs={{2,0},{4,2},{6,4},{8,6},{10,8},{12,10},{14,12},{16,14},{18,16},{20... | collective-permute-start | bytes 98312 | tf_op jit(solution)/shard_map/ppermute | solution.py:201
  108.8 3.5 %collective-permute-done.1 = s32[8,1024]{1,0:T(8,128)S(1)} collective-permute-done((s32[8,1024]{1,0:T(8,128)S(1)}, s32[8,1024]{1,0:T(8,128)S(1)}, u32[]{:S(2)}, u32[]{:S(2)}) %collective-permute-start.1) | collective-permute-done | bytes 32800 | tf_op jit(solution)/shard_map/ppermute | solution.py:201
  112.5 2.1 %collective-permute-start.5 = (f32[3,16,1024]{2,1,0:T(8,128)S(1)}, f32[3,16,1024]{2,1,0:T(8,128)S(1)}, u32[]{:S(2)}, u32[]{:S(2)}) collective-permute-start(f32[3,16,1024]{2,1,0:T(8,128)S(1)} %slice_divide_fusion.2.refs_4_), channel_id=1, source_target_pairs={{0,2},{2,4},{4,6},{6,8},{8,10},{10,12},{12,14},{14,16},{16,18},{18... | collective-permute-start | bytes 589832 | tf_op jit(solution)/shard_map/ppermute | solution.py:226
  114.6 0.1 add.39
  114.7 0.1 add.41
  114.9 0.1 slice_divide_fusion.refs_2_
  114.9 2.3 %collective-permute-start.7 = (f32[8,16,1024]{2,1,0:T(8,128)S(1)}, f32[8,16,1024]{2,1,0:T(8,128)S(1)}, u32[]{:S(2)}, u32[]{:S(2)}) collective-permute-start(f32[8,16,1024]{2,1,0:T(8,128)S(1)} %slice_divide_fusion.refs_2_), channel_id=1, source_target_pairs={{2,0},{4,2},{6,4},{8,6},{10,8},{12,10},{14,12},{16,14},{18,16},{20... | collective-permute-start | bytes 1572872 | tf_op jit(solution)/shard_map/ppermute | solution.py:224
  117.2 5.1 %collective-permute-start.3 = (f32[5,16,1024]{2,1,0:T(8,128)S(1)}, f32[5,16,1024]{2,1,0:T(8,128)S(1)}, u32[]{:S(2)}, u32[]{:S(2)}) collective-permute-start(f32[5,16,1024]{2,1,0:T(8,128)S(1)} %slice_divide_fusion.1.refs_3_), channel_id=1, source_target_pairs={{0,2},{2,4},{4,6},{6,8},{8,10},{10,12},{12,14},{14,16},{16,18},{18... | collective-permute-start | bytes 983048 | tf_op jit(solution)/shard_map/ppermute | solution.py:226
  122.3 0.1 multiply_bitcast_fusion
  122.5 0.1 broadcast_in_dim.23.inverse_ref
  122.6 0.1 copy.21.gain_ref
  122.8 0.1 add_convert_fusion.land_ref
  122.9 8.1 %collective-permute-done.3.refs_0_ = f32[5,16,1024]{2,1,0:T(8,128)S(1)} collective-permute-done((f32[5,16,1024]{2,1,0:T(8,128)S(1)}, f32[5,16,1024]{2,1,0:T(8,128)S(1)}, u32[]{:S(2)}, u32[]{:S(2)}) %collective-permute-start.3) | collective-permute-done | bytes 327712 | tf_op jit(solution)/shard_map/ppermute | solution.py:226
  131.1 12.6 %shard_map.59 = f32[16,16,1024]{2,1,0:T(8,128)S(1)} custom-call(f32[32,1,1024]{2,1,0:T(1,128)S(1)} %add_convert_fusion.land_ref, f32[32,1,1024]{2,1,0:T(1,128)S(1)} %copy.21.gain_ref, f32[32,1,1024]{2,1,0:T(1,128)S(1)} %broadcast_in_dim.23.inverse_ref, f32[5,16,1024]{2,1,0:T(8,128)S(1)} %collective-permute-done.3.refs_0_, ...), custom_call_target="tpu_custom_call" | custom-call | tf_op jit(solution)/shard_map/pallas_call | solution.py:230
  143.7 1.6 %copy.22 = f32[16,16,1024]{2,1,0:T(8,128)} copy(f32[16,16,1024]{2,0,1:T(8,128)S(1)} %bitcast.34) | data formatting | bytes 2097152 | tf_op jit(solution)/shard_map/transpose | solution.py:236
  (30 shorter events, 0.3 us)
Async XLA Ops:
  0.0 1.6 %copy-start.4 = (f32[4096]{0:T(1024)S(1)}, f32[4096]{0:T(1024)}, u32[]{:S(2)}) copy-start(f32[4096]{0:T(1024)} %param.7) | copy-start | bytes 49156
  1.2 5.2 %copy-start.3 = (bf16[4,4096]{1,0:T(4,128)(2,1)S(1)}, bf16[4,4096]{1,0:T(4,128)(2,1)}, u32[]{:S(2)}) copy-start(bf16[4,4096]{1,0:T(4,128)(2,1)} %param.6) | copy-start | bytes 98308
  24.2 2.0 %copy-start.1 = (bf16[64,16,1024]{2,1,0:T(8,128)(2,1)S(1)}, bf16[64,16,1024]{2,1,0:T(8,128)(2,1)}, u32[]{:S(2)}) copy-start(bf16[64,16,1024]{2,1,0:T(8,128)(2,1)} %param.5) | copy-start | bytes 6291460
  35.9 1.2 copy-start
  67.9 46.7 %collective-permute-start.6 = (f32[8,24,1024]{2,1,0:T(8,128)S(1)}, f32[8,24,1024]{2,1,0:T(8,128)S(1)}, u32[]{:S(2)}, u32[]{:S(2)}) collective-permute-start(f32[8,24,1024]{2,1,0:T(8,128)S(1)} %get-tuple-element.16), channel_id=1, source_target_pairs={{0,1},{1,0},{2,3},{3,2},{4,5},{5,4},{6,7},{7,6},{8,9},{9,8},{10,11... | collective-permute-start | bytes 2359304 | tf_op jit(solution)/shard_map/ppermute | solution.py:220
  80.9 20.9 %copy-start.2 = (s32[16,1024]{1,0:T(8,128)S(1)}, s32[16,1024]{1,0:T(8,128)}, u32[]{:S(2)}) copy-start(s32[16,1024]{1,0:T(8,128)} %param.9) | copy-start | bytes 196612
  80.9 31.5 %collective-permute-start.4 = (f32[3,24,1024]{2,1,0:T(8,128)S(1)}, f32[3,24,1024]{2,1,0:T(8,128)S(1)}, u32[]{:S(2)}, u32[]{:S(2)}) collective-permute-start(f32[3,24,1024]{2,1,0:T(8,128)S(1)} %get-tuple-element.14), channel_id=1, source_target_pairs={{0,1},{1,0},{2,3},{3,2},{4,5},{5,4},{6,7},{7,6},{8,9},{9,8},{10,11... | collective-permute-start | bytes 884744 | tf_op jit(solution)/shard_map/ppermute | solution.py:220
  100.5 14.0 %collective-permute-start.2 = (f32[5,24,1024]{2,1,0:T(8,128)S(1)}, f32[5,24,1024]{2,1,0:T(8,128)S(1)}, u32[]{:S(2)}, u32[]{:S(2)}) collective-permute-start(f32[5,24,1024]{2,1,0:T(8,128)S(1)} %get-tuple-element.12), channel_id=1, source_target_pairs={{0,1},{1,0},{2,3},{3,2},{4,5},{5,4},{6,7},{7,6},{8,9},{9,8},{10,11... | collective-permute-start | bytes 1474568 | tf_op jit(solution)/shard_map/ppermute | solution.py:220
  101.8 7.0 %collective-permute-start = (s32[8,1024]{1,0:T(8,128)S(1)}, s32[8,1024]{1,0:T(8,128)S(1)}, u32[]{:S(2)}, u32[]{:S(2)}) collective-permute-start(s32[8,1024]{1,0:T(8,128)S(1)} %get-tuple-element.19), channel_id=1, source_target_pairs={{0,2},{2,4},{4,6},{6,8},{8,10},{10,12},{12,14},{14,16},{16,18},{18... | collective-permute-start | bytes 98312 | tf_op jit(solution)/shard_map/ppermute | solution.py:200
  106.8 5.5 %collective-permute-start.1 = (s32[8,1024]{1,0:T(8,128)S(1)}, s32[8,1024]{1,0:T(8,128)S(1)}, u32[]{:S(2)}, u32[]{:S(2)}) collective-permute-start(s32[8,1024]{1,0:T(8,128)S(1)} %get-tuple-element.20), channel_id=1, source_target_pairs={{2,0},{4,2},{6,4},{8,6},{10,8},{12,10},{14,12},{16,14},{18,16},{20... | collective-permute-start | bytes 98312 | tf_op jit(solution)/shard_map/ppermute | solution.py:201
  112.5 10.4 %collective-permute-start.5 = (f32[3,16,1024]{2,1,0:T(8,128)S(1)}, f32[3,16,1024]{2,1,0:T(8,128)S(1)}, u32[]{:S(2)}, u32[]{:S(2)}) collective-permute-start(f32[3,16,1024]{2,1,0:T(8,128)S(1)} %slice_divide_fusion.2.refs_4_), channel_id=1, source_target_pairs={{0,2},{2,4},{4,6},{6,8},{8,10},{10,12},{12,14},{14,16},{16,18},{18... | collective-permute-start | bytes 589832 | tf_op jit(solution)/shard_map/ppermute | solution.py:226
  114.9 16.2 %collective-permute-start.7 = (f32[8,16,1024]{2,1,0:T(8,128)S(1)}, f32[8,16,1024]{2,1,0:T(8,128)S(1)}, u32[]{:S(2)}, u32[]{:S(2)}) collective-permute-start(f32[8,16,1024]{2,1,0:T(8,128)S(1)} %slice_divide_fusion.refs_2_), channel_id=1, source_target_pairs={{2,0},{4,2},{6,4},{8,6},{10,8},{12,10},{14,12},{16,14},{18,16},{20... | collective-permute-start | bytes 1572872 | tf_op jit(solution)/shard_map/ppermute | solution.py:224
  117.2 13.8 %collective-permute-start.3 = (f32[5,16,1024]{2,1,0:T(8,128)S(1)}, f32[5,16,1024]{2,1,0:T(8,128)S(1)}, u32[]{:S(2)}, u32[]{:S(2)}) collective-permute-start(f32[5,16,1024]{2,1,0:T(8,128)S(1)} %slice_divide_fusion.1.refs_3_), channel_id=1, source_target_pairs={{0,2},{2,4},{4,6},{6,8},{8,10},{10,12},{12,14},{14,16},{16,18},{18... | collective-permute-start | bytes 983048 | tf_op jit(solution)/shard_map/ppermute | solution.py:226
where the time goes:
time: 146 us; the launch traced here: 145 us
  Pallas kernels  90.3 us (62%)
  local copies, waits for them, and re-layouts  20.2 us (14%)
  starting transfers between devices  19.3 us (13%)
  waiting for transfers between devices  11.7 us (8%)
  other arithmetic  3.42 us (2%)
    pallas_call x3, Pallas kernels, species_sums(): pl.pallas_call(functools.partial(sums_kernel, per, rows_per_group), grid=...  61.7 us
    pallas_call x1, Pallas kernels, gather(): pl.pallas_call(functools.partial(gather_kernel, count), out_shape=jax.Sha...  16 us
    pallas_call x1, Pallas kernels, local(): pl.pallas_call(functools.partial(smooth_kernel, starts), out_shape=jax.Sh...  12.6 us
    ppermute x2, waiting for transfers between devices, local(): halo[first - (rows - SWEEPS)] = lax.ppermute(mean, 'cells', ahead)  8.15 us
    ppermute x2, starting transfers between devices, local(): halo[first - (rows - SWEEPS)] = lax.ppermute(mean, 'cells', ahead)  7.15 us
    concatenate x1, local copies, waits for them, and re-layouts, local(): jnp.concatenate([gathered * jnp.asarray(0.5, BF16), jnp.stack([high, midd...  6.68 us
    ppermute x1, starting transfers between devices, local(): below = lax.ppermute(land_weight[-SWEEPS:], 'cells', ahead)  5.05 us
    another operation x3, local copies, waits for them, and re-layouts, local(): jnp.stack([high, middle, low]).astype(BF16)  4.77 us
  transfers between devices with their start and end apart: 8, of which 2 were waited for; matrix products, arithmetic and copies ran while one was open for 1% of the time, Pallas kernels for 21%

commit v1 on v0

--- a/solution.py
+++ b/solution.py
@@ -211,6 +211,9 @@
     chunks = [(0, SWEEPS), (SWEEPS, rows - SWEEPS - last), (rows - last, last)]
     own, halo = {}, {}
     for first, size in [c for c in chunks if c[1]]:
+        if first > SWEEPS:
+            trait_blocks, own[SWEEPS] = lax.optimization_barrier((trait_blocks, own[SWEEPS]))
+            halo[SWEEPS + rows] = lax.ppermute(own[SWEEPS], "cells", back)
         sums = species_sums(
             cov_ext, w, trait_blocks, first, size, cols, per, groups, rows_per_group
         )
@@ -220,7 +223,7 @@
             whole = whole + lax.ppermute(sums[shift], "species", perm)
         mean = whole[:, :per] / whole[:, per : per + 1]
         own[SWEEPS + first] = mean
-        if first < SWEEPS:
+        if first < SWEEPS and not last:
             halo[SWEEPS + rows + first] = lax.ppermute(mean, "cells", back)
         if first >= rows - SWEEPS:
             halo[first - (rows - SWEEPS)] = lax.ppermute(mean, "cells", ahead)

time: 146 us -> 143 us (0.979)
  waiting for transfers between devices: 11.7 us -> 6.63 us
  starting transfers between devices: 19.3 us -> 21.4 us
    ppermute x1, waiting for transfers between devices: 3.53 us -> 0.01 us  [local(): above = lax.ppermute(land_weight[:SWEEPS], 'cells', back)]
    ppermute x2, starting transfers between devices: 7.15 us -> 9.85 us  [local(): halo[first - (rows - SWEEPS)] = lax.ppermute(mean, 'cells', ahead)]
    ppermute x2, waiting for transfers between devices: 8.15 us -> 6.62 us  [local(): halo[first - (rows - SWEEPS)] = lax.ppermute(mean, 'cells', ahead)]
  transfers between devices with their start and end apart: 8 -> 8, of which waited for: 2 -> 1; matrix products, arithmetic and copies ran while one was open for 1% -> 1% of each run, Pallas kernels for 21% -> 22%
where the time goes in v1:
time: 143 us
  Pallas kernels  90.6 us (63%)
  starting transfers between devices  21.4 us (15%)
  local copies, waits for them, and re-layouts  20.2 us (14%)
  waiting for transfers between devices  6.63 us (5%)
  other arithmetic  3.42 us (2%)
    pallas_call x3, Pallas kernels, species_sums(): pl.pallas_call(functools.partial(sums_kernel, per, rows_per_group), grid=...  61.9 us
    pallas_call x1, Pallas kernels, gather(): pl.pallas_call(functools.partial(gather_kernel, count), out_shape=jax.Sha...  16 us
    pallas_call x1, Pallas kernels, local(): pl.pallas_call(functools.partial(smooth_kernel, starts), out_shape=jax.Sh...  12.6 us
    ppermute x2, starting transfers between devices, local(): halo[first - (rows - SWEEPS)] = lax.ppermute(mean, 'cells', ahead)  9.85 us
    concatenate x1, local copies, waits for them, and re-layouts, local(): jnp.concatenate([gathered * jnp.asarray(0.5, BF16), jnp.stack([high, midd...  6.68 us
    ppermute x2, waiting for transfers between devices, local(): halo[first - (rows - SWEEPS)] = lax.ppermute(mean, 'cells', ahead)  6.62 us
    another operation x3, local copies, waits for them, and re-layouts, local(): jnp.stack([high, middle, low]).astype(BF16)  4.77 us
    ppermute x1, starting transfers between devices, local(): below = lax.ppermute(land_weight[-SWEEPS:], 'cells', ahead)  4.74 us
  transfers between devices with their start and end apart: 8, of which 1 were waited for; matrix products, arithmetic and copies ran while one was open for 1% of the time, Pallas kernels for 22%

profile of v1, /device:TPU:1, one launch (start us, length us, event | category | flops | bytes accessed | tf_op | source)
XLA Modules:
  0.0 142.6 jit_solution(15349391525715817559)
XLA Ops:
  0.0 0.1 pad.7.clone
  0.1 0.1 pad.6.clone
  0.2 1.0 fusion
  1.2 0.0 copy-start.3
  1.2 0.1 maximum_maximum_fusion.1
  1.4 0.1 copy.28
  1.5 0.1 copy.33
  1.6 1.6 %stack.17 = bf16[1,4096]{0,1:T(8,128)(2,1)} reshape(bf16[4096]{0:T(1024)(128)(2,1)S(1)} %get-tuple-element.27) | data formatting | bytes 16384 | tf_op jit(solution)/shard_map/stack | solution.py:175
  3.2 1.6 %stack.18 = bf16[1,4096]{0,1:T(8,128)(2,1)} reshape(bf16[4096]{0:T(1024)(128)(2,1)S(1)} %get-tuple-element.26) | data formatting | bytes 16384 | tf_op jit(solution)/shard_map/stack | solution.py:175
  4.8 1.6 %stack.19 = bf16[1,4096]{0,1:T(8,128)(2,1)} reshape(bf16[4096]{0:T(1024)(128)(2,1)S(1)} %get-tuple-element.25) | data formatting | bytes 16384 | tf_op jit(solution)/shard_map/stack | solution.py:175
  6.4 0.6 reshape.65.block_ref
  7.1 16.0 %shard_map.55 = bf16[16,16,1024]{2,1,0:T(8,128)(2,1)} custom-call(bf16[16,1024]{1,0:T(8,128)(2,1)} %reshape.65.block_ref), custom_call_target="tpu_custom_call" | custom-call | tf_op jit(solution)/shard_map/pallas_call | solution.py:143
  23.1 1.1 broadcast_multiply_fusion
  24.2 0.0 copy-start.1
  24.2 0.2 mul.35
  24.4 0.3 copy.15
  24.6 0.2 copy.27
  24.8 1.3 copy.16
  26.1 1.2 copy.26
  27.4 0.1 pad.11.clone
  27.4 0.1 pad.12.clone
  27.5 0.6 maximum_maximum_fusion.cov_ref
  28.1 1.1 broadcast_in_dim.26
  29.2 6.7 %concatenate.38 = bf16[80,4096]{0,1:T(8,128)(2,1)} concatenate(bf16[64,4096]{0,1:T(8,128)(2,1)} %copy.16, bf16[1,4096]{0,1:T(8,128)(2,1)} %stack.17, bf16[1,4096]{0,1:T(8,128)(2,1)} %stack.18, bf16[1,4096]{0,1:T(8,128)(2,1)} %stack.19, bf16[13,4096]{0,1:T(8,128)(2,1)} %broadcast_in_dim.26), dimensions={0} | concatenate | bytes 1310720 | tf_op jit(solution)/shard_map/concatenate | solution.py:172
  35.9 1.2 copy-done
  37.1 30.8 %shard_map.57 = (f32[8,24,1024]{2,1,0:T(8,128)S(1)}, f32[8,24,1024]{2,1,0:T(8,128)S(1)}) custom-call(bf16[80,16384]{1,0:T(8,128)(2,1)S(1)} %maximum_maximum_fusion.cov_ref, bf16[4096,80]{1,0:T(8,128)(2,1)S(1)} %bitcast.35, bf16[8,48,512]{2,1,0:T(8,128)(2,1)S(1)} %bitcast.38), custom_call_target="tpu_custom_call" | custom-call | flops 34359738368 | bytes 1572864 | tf_op jit(solution)/shard_map/pallas_call | solution.py:46
  67.9 0.0 copy-start.2
  68.0 1.3 collective-permute-start.4
  69.3 19.3 %shard_map.56 = (f32[5,24,1024]{2,1,0:T(8,128)S(1)}, f32[5,24,1024]{2,1,0:T(8,128)S(1)}) custom-call(bf16[80,16384]{1,0:T(8,128)(2,1)S(1)} %maximum_maximum_fusion.cov_ref, bf16[4096,80]{1,0:T(8,128)(2,1)S(1)} %bitcast.36, bf16[8,48,512]{2,1,0:T(8,128)(2,1)S(1)} %bitcast.39), custom_call_target="tpu_custom_call" | custom-call | flops 21474836480 | bytes 983040 | tf_op jit(solution)/shard_map/pallas_call | solution.py:46
  88.6 0.3 collective-permute-start.2
  88.9 4.7 %collective-permute-start = (s32[8,1024]{1,0:T(8,128)S(1)}, s32[8,1024]{1,0:T(8,128)S(1)}, u32[]{:S(2)}, u32[]{:S(2)}) collective-permute-start(s32[8,1024]{1,0:T(8,128)S(1)} %get-tuple-element.23), channel_id=1, source_target_pairs={{0,2},{2,4},{4,6},{6,8},{8,10},{10,12},{12,14},{14,16},{16,18},{18... | collective-permute-start | bytes 98312 | tf_op jit(solution)/shard_map/ppermute | solution.py:200
  93.7 1.9 %collective-permute-start.1 = (s32[8,1024]{1,0:T(8,128)S(1)}, s32[8,1024]{1,0:T(8,128)S(1)}, u32[]{:S(2)}, u32[]{:S(2)}) collective-permute-start(s32[8,1024]{1,0:T(8,128)S(1)} %get-tuple-element.24), channel_id=1, source_target_pairs={{2,0},{4,2},{6,4},{8,6},{10,8},{12,10},{14,12},{16,14},{18,16},{20... | collective-permute-start | bytes 98312 | tf_op jit(solution)/shard_map/ppermute | solution.py:201
  95.6 0.0 collective-permute-done.4
  95.7 0.1 add.40
  95.8 0.1 slice_divide_fusion.refs_2_
  95.9 11.9 %shard_map.58 = (f32[3,24,1024]{2,1,0:T(8,128)S(1)}, f32[3,24,1024]{2,1,0:T(8,128)S(1)}) custom-call(bf16[80,16384]{1,0:T(8,128)(2,1)S(1)} %maximum_maximum_fusion.cov_ref, bf16[4096,80]{1,0:T(8,128)(2,1)S(1)} %bitcast.37, bf16[8,48,512]{2,1,0:T(8,128)(2,1)S(1)} %bitcast.40), custom_call_target="tpu_custom_call" | custom-call | flops 12884901888 | bytes 589824 | tf_op jit(solution)/shard_map/pallas_call | solution.py:46
  107.7 1.3 collective-permute-start.5
  109.1 0.1 add.39
  109.2 3.9 %collective-permute-start.3 = (f32[5,16,1024]{2,1,0:T(8,128)S(1)}, f32[5,16,1024]{2,1,0:T(8,128)S(1)}, u32[]{:S(2)}, u32[]{:S(2)}) collective-permute-start(f32[5,16,1024]{2,1,0:T(8,128)S(1)} %slice_divide_fusion.1.refs_3_), channel_id=1, source_target_pairs={{0,2},{2,4},{4,6},{6,8},{8,10},{10,12},{12,14},{14,16},{16,18},{18... | collective-permute-start | bytes 983048 | tf_op jit(solution)/shard_map/ppermute | solution.py:229
  113.2 1.9 %collective-permute-start.7 = (f32[8,16,1024]{2,1,0:T(8,128)S(1)}, f32[8,16,1024]{2,1,0:T(8,128)S(1)}, u32[]{:S(2)}, u32[]{:S(2)}) collective-permute-start(f32[8,16,1024]{2,1,0:T(8,128)S(1)} %slice_divide_fusion.refs_2_), channel_id=1, source_target_pairs={{2,0},{4,2},{6,4},{8,6},{10,8},{12,10},{14,12},{16,14},{18,16},{20... | collective-permute-start | bytes 1572872 | tf_op jit(solution)/shard_map/ppermute | solution.py:216
  115.2 5.9 %collective-permute-start.6 = (f32[3,16,1024]{2,1,0:T(8,128)S(1)}, f32[3,16,1024]{2,1,0:T(8,128)S(1)}, u32[]{:S(2)}, u32[]{:S(2)}) collective-permute-start(f32[3,16,1024]{2,1,0:T(8,128)S(1)} %slice_divide_fusion.2.refs_4_), channel_id=1, source_target_pairs={{0,2},{2,4},{4,6},{6,8},{8,10},{10,12},{12,14},{14,16},{16,18},{18... | collective-permute-start | bytes 589832 | tf_op jit(solution)/shard_map/ppermute | solution.py:229
  121.1 0.1 multiply_bitcast_fusion
  121.3 0.1 broadcast_in_dim.23.inverse_ref
  121.4 0.1 copy.21.gain_ref
  121.6 0.1 add_convert_fusion.land_ref
  121.7 6.6 %collective-permute-done.6.refs_1_ = f32[3,16,1024]{2,1,0:T(8,128)S(1)} collective-permute-done((f32[3,16,1024]{2,1,0:T(8,128)S(1)}, f32[3,16,1024]{2,1,0:T(8,128)S(1)}, u32[]{:S(2)}, u32[]{:S(2)}) %collective-permute-start.6) | collective-permute-done | bytes 196640 | tf_op jit(solution)/shard_map/ppermute | solution.py:229
  128.4 12.6 %shard_map.59 = f32[16,16,1024]{2,1,0:T(8,128)S(1)} custom-call(f32[32,1,1024]{2,1,0:T(1,128)S(1)} %add_convert_fusion.land_ref, f32[32,1,1024]{2,1,0:T(1,128)S(1)} %copy.21.gain_ref, f32[32,1,1024]{2,1,0:T(1,128)S(1)} %broadcast_in_dim.23.inverse_ref, f32[5,16,1024]{2,1,0:T(8,128)S(1)} %collective-permute-done.3.refs_0_, ...), custom_call_target="tpu_custom_call" | custom-call | tf_op jit(solution)/shard_map/pallas_call | solution.py:233
  141.0 1.6 %copy.22 = f32[16,16,1024]{2,1,0:T(8,128)} copy(f32[16,16,1024]{2,0,1:T(8,128)S(1)} %bitcast.34) | data formatting | bytes 2097152 | tf_op jit(solution)/shard_map/transpose | solution.py:239
  (30 shorter events, 0.3 us)
Async XLA Ops:
  0.0 1.6 %copy-start.4 = (f32[4096]{0:T(1024)S(1)}, f32[4096]{0:T(1024)}, u32[]{:S(2)}) copy-start(f32[4096]{0:T(1024)} %param.7) | copy-start | bytes 49156
  1.2 5.2 %copy-start.3 = (bf16[4,4096]{1,0:T(4,128)(2,1)S(1)}, bf16[4,4096]{1,0:T(4,128)(2,1)}, u32[]{:S(2)}) copy-start(bf16[4,4096]{1,0:T(4,128)(2,1)} %param.6) | copy-start | bytes 98308
  24.2 2.0 %copy-start.1 = (bf16[64,16,1024]{2,1,0:T(8,128)(2,1)S(1)}, bf16[64,16,1024]{2,1,0:T(8,128)(2,1)}, u32[]{:S(2)}) copy-start(bf16[64,16,1024]{2,1,0:T(8,128)(2,1)} %param.5) | copy-start | bytes 6291460
  35.9 1.2 copy-start
  67.9 21.0 %copy-start.2 = (s32[16,1024]{1,0:T(8,128)S(1)}, s32[16,1024]{1,0:T(8,128)}, u32[]{:S(2)}) copy-start(s32[16,1024]{1,0:T(8,128)} %param.9) | copy-start | bytes 196612
  68.0 27.7 %collective-permute-start.4 = (f32[8,24,1024]{2,1,0:T(8,128)S(1)}, f32[8,24,1024]{2,1,0:T(8,128)S(1)}, u32[]{:S(2)}, u32[]{:S(2)}) collective-permute-start(f32[8,24,1024]{2,1,0:T(8,128)S(1)} %get-tuple-element.16), channel_id=1, source_target_pairs={{0,1},{1,0},{2,3},{3,2},{4,5},{5,4},{6,7},{7,6},{8,9},{9,8},{10,11... | collective-permute-start | bytes 2359304 | tf_op jit(solution)/shard_map/ppermute | solution.py:223
  88.6 20.5 %collective-permute-start.2 = (f32[5,24,1024]{2,1,0:T(8,128)S(1)}, f32[5,24,1024]{2,1,0:T(8,128)S(1)}, u32[]{:S(2)}, u32[]{:S(2)}) collective-permute-start(f32[5,24,1024]{2,1,0:T(8,128)S(1)} %get-tuple-element.14), channel_id=1, source_target_pairs={{0,1},{1,0},{2,3},{3,2},{4,5},{5,4},{6,7},{7,6},{8,9},{9,8},{10,11... | collective-permute-start | bytes 1474568 | tf_op jit(solution)/shard_map/ppermute | solution.py:223
  88.9 20.2 %collective-permute-start = (s32[8,1024]{1,0:T(8,128)S(1)}, s32[8,1024]{1,0:T(8,128)S(1)}, u32[]{:S(2)}, u32[]{:S(2)}) collective-permute-start(s32[8,1024]{1,0:T(8,128)S(1)} %get-tuple-element.23), channel_id=1, source_target_pairs={{0,2},{2,4},{4,6},{6,8},{8,10},{10,12},{12,14},{14,16},{16,18},{18... | collective-permute-start | bytes 98312 | tf_op jit(solution)/shard_map/ppermute | solution.py:200
  93.7 15.4 %collective-permute-start.1 = (s32[8,1024]{1,0:T(8,128)S(1)}, s32[8,1024]{1,0:T(8,128)S(1)}, u32[]{:S(2)}, u32[]{:S(2)}) collective-permute-start(s32[8,1024]{1,0:T(8,128)S(1)} %get-tuple-element.24), channel_id=1, source_target_pairs={{2,0},{4,2},{6,4},{8,6},{10,8},{12,10},{14,12},{16,14},{18,16},{20... | collective-permute-start | bytes 98312 | tf_op jit(solution)/shard_map/ppermute | solution.py:201
  107.7 7.4 %collective-permute-start.5 = (f32[3,24,1024]{2,1,0:T(8,128)S(1)}, f32[3,24,1024]{2,1,0:T(8,128)S(1)}, u32[]{:S(2)}, u32[]{:S(2)}) collective-permute-start(f32[3,24,1024]{2,1,0:T(8,128)S(1)} %get-tuple-element.19), channel_id=1, source_target_pairs={{0,1},{1,0},{2,3},{3,2},{4,5},{5,4},{6,7},{7,6},{8,9},{9,8},{10,11... | collective-permute-start | bytes 884744 | tf_op jit(solution)/shard_map/ppermute | solution.py:223
  109.2 12.5 %collective-permute-start.3 = (f32[5,16,1024]{2,1,0:T(8,128)S(1)}, f32[5,16,1024]{2,1,0:T(8,128)S(1)}, u32[]{:S(2)}, u32[]{:S(2)}) collective-permute-start(f32[5,16,1024]{2,1,0:T(8,128)S(1)} %slice_divide_fusion.1.refs_3_), channel_id=1, source_target_pairs={{0,2},{2,4},{4,6},{6,8},{8,10},{10,12},{12,14},{14,16},{16,18},{18... | collective-permute-start | bytes 983048 | tf_op jit(solution)/shard_map/ppermute | solution.py:229
  113.2 15.2 %collective-permute-start.7 = (f32[8,16,1024]{2,1,0:T(8,128)S(1)}, f32[8,16,1024]{2,1,0:T(8,128)S(1)}, u32[]{:S(2)}, u32[]{:S(2)}) collective-permute-start(f32[8,16,1024]{2,1,0:T(8,128)S(1)} %slice_divide_fusion.refs_2_), channel_id=1, source_target_pairs={{2,0},{4,2},{6,4},{8,6},{10,8},{12,10},{14,12},{16,14},{18,16},{20... | collective-permute-start | bytes 1572872 | tf_op jit(solution)/shard_map/ppermute | solution.py:216
  115.2 13.1 %collective-permute-start.6 = (f32[3,16,1024]{2,1,0:T(8,128)S(1)}, f32[3,16,1024]{2,1,0:T(8,128)S(1)}, u32[]{:S(2)}, u32[]{:S(2)}) collective-permute-start(f32[3,16,1024]{2,1,0:T(8,128)S(1)} %slice_divide_fusion.2.refs_4_), channel_id=1, source_target_pairs={{0,2},{2,4},{4,6},{6,8},{8,10},{10,12},{12,14},{14,16},{16,18},{18... | collective-permute-start | bytes 589832 | tf_op jit(solution)/shard_map/ppermute | solution.py:229
